TPU v7x, 512 devices: a whole 4x8x8 slice. The times are simulated.
512 devices in a mesh: seq: 64 (over z_hi, y, core), chan: 8 (over x, z_lo).
Axes of the slice: x: 4, y: 8, z: 8 (z_hi: 4, z_lo: 2; z = z_hi * 2 + z_lo), core: 2. Of those that a mesh axis runs over, the one named last changes fastest.
Arguments:
- inputs: bfloat16 [65536, 2048], P('seq', 'chan'), may hold values from -6 to 6
- out_grad: bfloat16 [65536, 2048], P('seq', 'chan'), may hold values from -6 to 6
- kernel: bfloat16 [64, 1024, 2048], P(None, 'seq', 'chan'), may hold values from -6 to 6
- inner_factor: bfloat16 [1024, 1024], replicated, may hold values from -0.1875 to 0.1875
- outer_factor: float32 [64, 64], replicated, may hold values from -0.75 to 0.75
- chan_blocks: bfloat16 [8, 256, 256], P('chan'), may hold values from -0.375 to 0.375
- chan_mixers: bfloat16 [256, 8, 8], replicated, may hold values from -2 to 2
Outputs:
- mixed: bfloat16 [65536, 2048], P('seq', 'chan')
- in_grad: bfloat16 [65536, 2048], P('seq', 'chan')
- kernel_grad: bfloat16 [64, 1024, 2048], P(None, 'seq', 'chan')
All inputs are finite; a program needn't handle non-finite values.
Results may differ from a plain program's by a relative error of at most 0.014.
Values may be sent and summed in bfloat16 or wider, within the bound.
A program may use at most 64 MiB of HBM per device.

v0:
```python
import jax
import jax.numpy as jnp
from jax import lax
from jax.sharding import PartitionSpec as P

BLK = 1024


HIGH = lax.Precision.HIGHEST


def local(inputs, out_grad, kernel, inner_factor, outer_factor, chan_blocks, chan_mixers):
    f32 = jnp.float32
    bf16 = jnp.bfloat16
    tok_rows = inputs.shape[0]
    chan_dev = inputs.shape[1]
    grid_rows = tok_rows // BLK
    groups_dev = chan_blocks.shape[0]
    block_size = chan_blocks.shape[1]
    slice_size = block_size // lax.axis_size("chan")
    chan_index = lax.axis_index("chan")
    gate = kernel.astype(f32)
    grid_x = inputs.reshape(grid_rows, BLK, chan_dev)
    first = jnp.einsum("ijc,jk->ikc", grid_x, inner_factor, preferred_element_type=f32)
    first_cols = lax.all_to_all(first, "seq", split_axis=1, concat_axis=0, tiled=True)
    second = jnp.einsum("ai,ijc->ajc", outer_factor, first_cols, precision=HIGH)
    gated = second * gate
    back = jnp.einsum("ia,ijc->ajc", outer_factor, gated, precision=HIGH).astype(bf16)
    back_rows = lax.all_to_all(back, "seq", split_axis=0, concat_axis=1, tiled=True)
    ymat = jnp.einsum("ijc,kj->ikc", back_rows, inner_factor, preferred_element_type=f32).astype(
        bf16
    )
    yres = ymat.reshape(tok_rows, groups_dev, block_size)
    pmat = jnp.einsum("tgm,gmn->tgn", yres, chan_blocks, preferred_element_type=f32).astype(bf16)
    p_slices = lax.all_to_all(pmat, "chan", split_axis=2, concat_axis=1, tiled=True)
    mix_slice = lax.dynamic_slice_in_dim(chan_mixers, chan_index * slice_size, slice_size, 0)
    qmat = jnp.einsum("tgm,mhg->thm", p_slices, mix_slice, preferred_element_type=f32).astype(bf16)
    q_groups = lax.all_to_all(qmat, "chan", split_axis=1, concat_axis=2, tiled=True)
    mixed = (inputs.astype(f32) + q_groups.reshape(tok_rows, chan_dev).astype(f32)).astype(bf16)
    dq_res = out_grad.reshape(tok_rows, groups_dev, block_size)
    mix_local = lax.dynamic_slice_in_dim(chan_mixers, chan_index * groups_dev, groups_dev, 2)
    dp_mat = jnp.einsum(
        "thm,mhg->tgm",
        lax.all_gather(dq_res, "chan", axis=1, tiled=True),
        mix_local,
        preferred_element_type=f32,
    ).astype(bf16)
    dy_mat = jnp.einsum("tgn,gmn->tgm", dp_mat, chan_blocks, preferred_element_type=f32).astype(
        bf16
    )
    dy_grid = dy_mat.reshape(grid_rows, BLK, chan_dev)
    dc_mat = jnp.einsum("ikc,kj->ijc", dy_grid, inner_factor, preferred_element_type=f32)
    dc_cols = lax.all_to_all(
        dc_mat.astype(jnp.bfloat16), "seq", split_axis=1, concat_axis=0, tiled=True
    ).astype(dc_mat.dtype)
    dg_mat = jnp.einsum("ai,ijc->ajc", outer_factor, dc_cols, precision=HIGH)
    kernel_grad = (dg_mat * second).astype(bf16)
    da_mat = jnp.einsum("ai,ajc->ijc", outer_factor, dg_mat * gate, precision=HIGH).astype(bf16)
    da_rows = lax.all_to_all(da_mat, "seq", split_axis=0, concat_axis=1, tiled=True)
    dx_mat = jnp.einsum("ikc,jk->ijc", da_rows, inner_factor, preferred_element_type=f32)
    in_grad = (out_grad.astype(f32) + dx_mat.reshape(tok_rows, chan_dev)).astype(bf16)
    return (mixed, in_grad, kernel_grad)


def solution(mesh):
    in_specs = (
        P("seq", "chan"),
        P("seq", "chan"),
        P(None, "seq", "chan"),
        P(),
        P(),
        P("chan", None, None),
        P(),
    )
    out_specs = (P("seq", "chan"), P("seq", "chan"), P(None, "seq", "chan"))
    return jax.shard_map(local, mesh=mesh, in_specs=in_specs, out_specs=out_specs, check_vma=False)
```

profile of v0, /device:TPU:1, one launch (start us, length us, event | category | flops | bytes accessed | tf_op | source)
XLA Modules:
  0.0 256.4 jit_solution(3915622956640849107)
XLA Ops:
  8.8 1.8 convolution_bitcast_fusion.2
  11.6 47.0 %all_to_all.63 = f32[1,1024,256]{2,0,1:T(1,128)S(1)} all-to-all(f32[1,1024,256]{2,0,1:T(1,128)S(1)} %copy.58), channel_id=1, replica_groups=mesh['seq'=64,'chan'=8] {'seq'}, dimensions={1} | all-to-all | bytes 2097152 | tf_op jit(solution)/shard_map/all_to_all | solution.py:25
  58.8 1.7 convolution_bitcast_fusion.3
  62.8 8.9 %all-to-all-start.1 = ((bf16[64,16,256]{2,1,0:T(8,128)(2,1)}), bf16[64,16,256]{2,1,0:T(8,128)(2,1)}, u32[]{:S(2)}, u32[]{:S(2)}) async-start(bf16[64,16,256]{2,1,0:T(8,128)(2,1)} %copy.62), calls=%async_computation.1 | async-start | bytes 1048576 | tf_op jit(solution)/shard_map/all_to_all | solution.py:29
  71.8 18.5 %all-to-all-done.1 = bf16[64,16,256]{2,1,0:T(8,128)(2,1)} async-done(((bf16[64,16,256]{2,1,0:T(8,128)(2,1)}), bf16[64,16,256]{2,1,0:T(8,128)(2,1)}, u32[]{:S(2)}, u32[]{:S(2)}) %all-to-all-start.1) | async-done | bytes 524320 | tf_op jit(solution)/shard_map/all_to_all | solution.py:29
  90.3 2.9 %fusion.4 = bf16[1024,1,256]{2,0,1:T(8,128)(2,1)} fusion(bf16[1024,256]{1,0:T(8,128)(2,1)} %bitcast.6, bf16[1024,1024]{1,0:T(8,128)(2,1)S(1)} %copy-done, bf16[1,256,256]{2,1,0:T(8,128)(2,1)S(1)} %copy-done.7), kind=kOutput, calls=%fused_computation.18 | convolution fusion | flops 671612928 | bytes 3276800 | tf_op jit(solution)/shard_map/tgm,gmn->tgn/dot_general | solution.py:34
  93.2 3.6 %copy.63 = bf16[1024,1,256]{0,1,2:T(2,128)(2,1)} copy(bf16[1024,1,256]{2,0,1:T(8,128)(2,1)} %fusion.4) | data formatting | bytes 1048576 | tf_op jit(solution)/shard_map/convert_element_type | solution.py:34
  97.3 5.6 %reduce.2 = bf16[256,1024]{1,0:T(8,128)(2,1)} reduce(bf16[256,1,1024]{2,1,0:T(2,128)(2,1)} %bitcast.86, bf16[]{:T(256)} %broadcast.1), dimensions={1}, to_apply=%bitcast.69.reduce_sub_computation | reduce | bytes 1048578
  102.9 2.2 reshape.88
  105.1 4.3 %all-to-all-start.2 = ((bf16[8,2,16384]{2,1,0:T(2,128)(2,1)}), bf16[8,2,16384]{2,1,0:T(2,128)(2,1)}, u32[]{:S(2)}, u32[]{:S(2)}) async-start(bf16[8,2,16384]{2,1,0:T(2,128)(2,1)} %reshape.88), calls=%async_computation.2 | async-start | bytes 1048576 | tf_op jit(solution)/shard_map/all_to_all | solution.py:35
  109.5 40.1 %all-gather.3.cloned.1.call-done = bf16[1024,2048]{1,0:T(8,128)(2,1)} async-done(((bf16[1024,256]{1,0:T(8,128)(2,1)}), bf16[1024,2048]{1,0:T(8,128)(2,1)}) %all-gather.3.cloned.1.call-update) | async-done | bytes 4194320 | tf_op jit(solution)/shard_map/all_gather | solution.py:44
  149.7 3.7 %copy.93 = bf16[128,8,8,256]{3,2,1,0:T(8,128)(2,1)S(1)} copy(bf16[128,8,8,256]{3,1,2,0:T(8,128)(2,1)} %bitcast.85) | data formatting | bytes 8388608
  153.3 4.1 %multiply_reduce_fusion = bf16[256,1024]{0,1:T(8,128)(2,1)} fusion(f32[256,8]{0,1:T(8,128)S(1)} %bitcast_convert_fusion, bf16[128,8,8,256]{3,2,1,0:T(8,128)(2,1)S(1)} %copy.93), kind=kLoop, calls=%fused_computation | loop fusion | flops 6029312 | bytes 4726784
  157.4 2.0 copy.81
  159.5 3.1 %fusion.3 = bf16[1,1024,256]{1,2,0:T(8,128)(2,1)} fusion(bf16[1024,1024]{1,0:T(8,128)(2,1)S(1)} %copy-done, bf16[256,1024]{1,0:T(8,128)(2,1)} %copy.81, bf16[1,256,256]{2,1,0:T(8,128)(2,1)S(1)} %copy-done.7), kind=kOutput, calls=%fused_computation.17 | convolution fusion | flops 671612928 | bytes 3276800 | tf_op jit(solution)/shard_map/ikc,kj->ijc/dot_general | solution.py:52
  162.6 3.6 %copy.68 = bf16[1,1024,256]{2,0,1:T(2,128)(2,1)} copy(bf16[1,1024,256]{1,2,0:T(8,128)(2,1)} %fusion.3) | data formatting | bytes 1048576 | tf_op jit(solution)/shard_map/convert_element_type | solution.py:54
  166.1 5.5 %reduce.3 = bf16[1024,256]{1,0:T(8,128)(2,1)} reduce(bf16[1024,1,256]{2,1,0:T(2,128)(2,1)} %bitcast.87, bf16[]{:T(256)} %broadcast.1), dimensions={1}, to_apply=%bitcast.71.reduce_sub_computation | reduce | bytes 1048578
  171.7 2.0 reshape.90
  173.6 12.1 %all-to-all-start.4 = ((bf16[64,2,2048]{2,1,0:T(2,128)(2,1)}), bf16[64,2,2048]{2,1,0:T(2,128)(2,1)}, u32[]{:S(2)}, u32[]{:S(2)}) async-start(bf16[64,2,2048]{2,1,0:T(2,128)(2,1)} %reshape.90), calls=%async_computation.4 | async-start | bytes 1048576 | tf_op jit(solution)/shard_map/all_to_all | solution.py:53
  186.0 3.5 %reshape.89 = bf16[256,1,1024]{2,1,0:T(2,128)(2,1)} reshape(bf16[8,2,16384]{2,1,0:T(2,128)(2,1)} %all-to-all-done.2) | data formatting | bytes 1048576
  189.4 1.4 copy.86
  192.3 12.1 %all-to-all-done.4 = bf16[64,2,2048]{2,1,0:T(2,128)(2,1)} async-done(((bf16[64,2,2048]{2,1,0:T(2,128)(2,1)}), bf16[64,2,2048]{2,1,0:T(2,128)(2,1)}, u32[]{:S(2)}, u32[]{:S(2)}) %all-to-all-start.4) | async-done | bytes 524320 | tf_op jit(solution)/shard_map/all_to_all | solution.py:53
  204.5 5.5 %all-to-all-start.3 = ((bf16[1024,8,32]{0,2,1:T(8,128)(2,1)}), bf16[1024,8,32]{0,2,1:T(8,128)(2,1)}, u32[]{:S(2)}, u32[]{:S(2)}) async-start(bf16[1024,8,32]{0,2,1:T(8,128)(2,1)} %copy.65), calls=%async_computation.3 | async-start | bytes 1048576 | tf_op jit(solution)/shard_map/all_to_all | solution.py:38
  210.0 4.4 %reshape.91 = bf16[1024,1,256]{2,1,0:T(2,128)(2,1)} reshape(bf16[64,2,2048]{2,1,0:T(2,128)(2,1)} %all-to-all-done.4) | data formatting | bytes 1048576
  214.4 1.4 copy.87
  215.8 1.4 multiply_convert_fusion
  219.5 8.6 %all-to-all-start.5 = ((bf16[64,16,256]{2,1,0:T(8,128)(2,1)}), bf16[64,16,256]{2,1,0:T(8,128)(2,1)}, u32[]{:S(2)}, u32[]{:S(2)}) async-start(bf16[64,16,256]{2,1,0:T(8,128)(2,1)} %copy.71), calls=%async_computation.5 | async-start | bytes 1048576 | tf_op jit(solution)/shard_map/all_to_all | solution.py:59
  229.5 2.1 copy.66
  231.6 2.0 fusion.7
  233.6 2.1 copy.72
  236.8 9.9 %all-to-all-done.5 = bf16[64,16,256]{2,1,0:T(8,128)(2,1)} async-done(((bf16[64,16,256]{2,1,0:T(8,128)(2,1)}), bf16[64,16,256]{2,1,0:T(8,128)(2,1)}, u32[]{:S(2)}, u32[]{:S(2)}) %all-to-all-start.5) | async-done | bytes 524320 | tf_op jit(solution)/shard_map/all_to_all | solution.py:59
  246.7 1.8 fusion.1
  (36 shorter events, 13.0 us)
Async XLA Ops:
  7.2 1.6 copy-start
  7.2 142.5 %all-gather.3.cloned.1.call-start = ((), (), s32[]{:S(2)}) async-start(), calls=%async_computation.6 | async-start | bytes 4718592 | tf_op jit(solution)/shard_map/all_gather | solution.py:44
  11.6 47.1 %copy-start.4 = (f32[64,64]{1,0:T(8,128)S(1)}, f32[64,64]{1,0:T(8,128)}, u32[]{:S(2)}) copy-start(f32[64,64]{1,0:T(8,128)} %param.11) | copy-start | bytes 49156
  58.7 1.8 copy-start.2
  60.5 29.8 %copy-start.7 = (bf16[1,256,256]{2,1,0:T(8,128)(2,1)S(1)}, bf16[1,256,256]{2,1,0:T(8,128)(2,1)}, u32[]{:S(2)}) copy-start(bf16[1,256,256]{2,1,0:T(8,128)(2,1)} %param.12) | copy-start | bytes 393220
  62.8 27.5 %all-to-all-start.1 = ((bf16[64,16,256]{2,1,0:T(8,128)(2,1)}), bf16[64,16,256]{2,1,0:T(8,128)(2,1)}, u32[]{:S(2)}, u32[]{:S(2)}) async-start(bf16[64,16,256]{2,1,0:T(8,128)(2,1)} %copy.62), calls=%async_computation.1 | async-start | bytes 1048576 | tf_op jit(solution)/shard_map/all_to_all | solution.py:29
  96.8 12.7 %copy-start.6 = (bf16[256,8,8]{0,2,1:T(8,128)(2,1)S(1)}, bf16[256,8,8]{0,2,1:T(8,128)(2,1)}, u32[]{:S(2)}) copy-start(bf16[256,8,8]{0,2,1:T(8,128)(2,1)} %param.13) | copy-start | bytes 98308
  105.1 68.5 %all-to-all-start.2 = ((bf16[8,2,16384]{2,1,0:T(2,128)(2,1)}), bf16[8,2,16384]{2,1,0:T(2,128)(2,1)}, u32[]{:S(2)}, u32[]{:S(2)}) async-start(bf16[8,2,16384]{2,1,0:T(2,128)(2,1)} %reshape.88), calls=%async_computation.2 | async-start | bytes 1048576 | tf_op jit(solution)/shard_map/all_to_all | solution.py:35
  173.6 30.8 %all-to-all-start.4 = ((bf16[64,2,2048]{2,1,0:T(2,128)(2,1)}), bf16[64,2,2048]{2,1,0:T(2,128)(2,1)}, u32[]{:S(2)}, u32[]{:S(2)}) async-start(bf16[64,2,2048]{2,1,0:T(2,128)(2,1)} %reshape.90), calls=%async_computation.4 | async-start | bytes 1048576 | tf_op jit(solution)/shard_map/all_to_all | solution.py:53
  204.5 15.1 %all-to-all-start.3 = ((bf16[1024,8,32]{0,2,1:T(8,128)(2,1)}), bf16[1024,8,32]{0,2,1:T(8,128)(2,1)}, u32[]{:S(2)}, u32[]{:S(2)}) async-start(bf16[1024,8,32]{0,2,1:T(8,128)(2,1)} %copy.65), calls=%async_computation.3 | async-start | bytes 1048576 | tf_op jit(solution)/shard_map/all_to_all | solution.py:38
  214.4 2.8 %copy-start.3 = (bf16[64,16,256]{2,1,0:T(8,128)(2,1)S(1)}, bf16[64,16,256]{2,1,0:T(8,128)(2,1)}, u32[]{:S(2)}) copy-start(bf16[64,16,256]{2,1,0:T(8,128)(2,1)} %param.9) | copy-start | bytes 1572868
  219.5 27.2 %all-to-all-start.5 = ((bf16[64,16,256]{2,1,0:T(8,128)(2,1)}), bf16[64,16,256]{2,1,0:T(8,128)(2,1)}, u32[]{:S(2)}, u32[]{:S(2)}) async-start(bf16[64,16,256]{2,1,0:T(8,128)(2,1)} %copy.71), calls=%async_computation.5 | async-start | bytes 1048576 | tf_op jit(solution)/shard_map/all_to_all | solution.py:59
  229.4 6.3 %copy-start.1 = (bf16[64,16,256]{2,0,1:T(8,128)(2,1)S(1)}, bf16[64,16,256]{2,0,1:T(8,128)(2,1)}, u32[]{:S(2)}) copy-start(bf16[64,16,256]{2,0,1:T(8,128)(2,1)} %get-tuple-element.15) | copy-start | bytes 1572868
  233.6 13.1 %copy-start.5 = (bf16[1024,256]{0,1:T(8,128)(2,1)S(1)}, bf16[1024,256]{0,1:T(8,128)(2,1)}, u32[]{:S(2)}) copy-start(bf16[1024,256]{0,1:T(8,128)(2,1)} %copy.66) | copy-start | bytes 1572868
Sparse Core Ops, SparseCore 0:
  10.0 139.5 all-gather.2
where the time goes:
time: 258 us; the launch traced here: 256 us
  waiting for transfers between devices  81.4 us (32%)
  blocking collectives  47 us (18%)
  local copies, waits for them, and re-layouts  41.3 us (16%)
  starting transfers between devices  39.6 us (15%)
  other arithmetic  17.2 us (7%)
  matrix products  15.6 us (6%)
  between operations  14.2 us (6%)
    all_to_all x1, blocking collectives, local(): lax.all_to_all(first, 'seq', split_axis=1, concat_axis=0, tiled=True)  47 us
    all_gather x1, waiting for transfers between devices, local(): lax.all_gather(dq_res, 'chan', axis=1, tiled=True)  40.1 us
    unnamed x31, local copies, waits for them, and re-layouts  27.7 us
    all_to_all x1, waiting for transfers between devices, local(): lax.all_to_all(back, 'seq', split_axis=0, concat_axis=1, tiled=True)  18.5 us
    unnamed x4, other arithmetic  15.2 us
    all_to_all x1, starting transfers between devices, local(): lax.all_to_all(dc_mat.astype(jnp.bfloat16), 'seq', split_axis=1, concat_a...  12.1 us
    all_to_all x1, waiting for transfers between devices, local(): lax.all_to_all(dc_mat.astype(jnp.bfloat16), 'seq', split_axis=1, concat_a...  12.1 us
    all_to_all x1, waiting for transfers between devices, local(): lax.all_to_all(da_mat, 'seq', split_axis=0, concat_axis=1, tiled=True)  9.94 us
  transfers between devices with their start and end apart: 6, of which 4 were waited for; matrix products, arithmetic and copies ran while one was open for 27% of the time, Pallas kernels for 0%

commit v1 on v0

v1 whole, which is shorter than its diff:
```python
import jax
import jax.numpy as jnp
from jax import lax
from jax.experimental import pallas as pl
from jax.experimental.pallas import tpu as pltpu
from jax.sharding import PartitionSpec as P

MESH = pl.DeviceIdType.MESH
F32 = jnp.float32
BF16 = jnp.bfloat16

ZH, YC, NX, NZ, NQ = 4, 16, 4, 8, 8
PLANE = NX * NZ


def mm(a, b, dims=((1,), (0,))):
    return lax.dot_general(a, b, (dims, ((), ())), preferred_element_type=F32)


def iota(shape, dim):
    return lax.broadcasted_iota(jnp.int32, shape, dim)


def kernel(
    x_ref, og_ref, gate_ref, inner_ref, outer_ref, blocks_ref, mix_ref,
    mixed_ref, ingrad_ref, kgrad_ref,
    a_buf, e_buf, fz, fy, b_buf, cc, fp, fm, fq, fa, fs, fr,
    by, bs, ba, bq, bm, bd, da, bt, bu,
    k_mat, kt_mat, w_blk, w_mix, w_perm,
    send, recv,
):
    s = lax.axis_index("seq")
    q = lax.axis_index("chan")
    zh, yc = s // YC, s % YC
    xx, zl = q // 2, q % 2
    zz = zh * 2 + zl

    def dev(zh_, yc_, q_):
        return (zh_ * YC + yc_, q_)

    def yc_peer(d):
        y = (yc // 2 + d // 2) % 8
        return y * 2 + (yc + d) % 2

    def plane_peer(d):
        z = (zz + d // NX) % NZ
        return z // 2, ((xx + d) % NX) * 2 + z % 2

    def chan_peer(d):
        return ((xx + d // 2) % NX) * 2 + (zl + d) % 2

    def put(src, dst, stage, to):
        pltpu.make_async_remote_copy(
            src_ref=src, dst_ref=dst, send_sem=send.at[stage], recv_sem=recv.at[stage],
            device_id=to, device_id_type=MESH,
        ).start()

    near = dev(zh, yc_peer(1), q)

    def taken(part, stage):
        pltpu.make_async_remote_copy(
            src_ref=part, dst_ref=part, send_sem=send.at[stage], recv_sem=recv.at[stage],
            device_id=near, device_id_type=MESH,
        ).wait_recv()

    def sent(part, stage):
        pltpu.make_async_remote_copy(
            src_ref=part, dst_ref=part, send_sem=send.at[stage], recv_sem=recv.at[stage],
            device_id=near, device_id_type=MESH,
        ).wait_send()

    def loop(n, body, start=0):
        def step(i, carry):
            body(i)
            return carry

        lax.fori_loop(start, n, step, 0)

    def rows(i, n=256):
        return pl.ds(pl.multiple_of(i * n, n), n)

    barrier = pltpu.get_barrier_semaphore()

    def greet_yc(d):
        pl.semaphore_signal(barrier, inc=1, device_id=dev(zh, yc_peer(d), q), device_id_type=MESH)

    def greet_plane(d):
        z_, q_ = plane_peer(d)
        pl.semaphore_signal(barrier, inc=1, device_id=dev(z_, yc, q_), device_id_type=MESH)

    loop(PLANE, greet_plane, 1)
    loop(YC, greet_yc, 1)

    def first(i):
        tall = inner_ref[:, rows(i)]
        a_buf[i] = mm(tall, x_ref[...], ((0,), (0,))).astype(BF16)
        e_buf[i] = mm(tall, og_ref[...], ((0,), (0,))).astype(BF16).reshape(YC, 16, 256)

    for i in range(ZH):
        first(i)

    pl.semaphore_wait(barrier, PLANE - 1 + YC - 1)

    def f1z(d):
        to = (zh + d) % ZH
        put(a_buf.at[to], fz.at[zh], 0, dev(to, yc, q))

    def b1(d):
        to = yc_peer(d)
        put(e_buf.at[:, to], by.at[yc], 1, dev(zh, to, q))

    loop(ZH, f1z, 1)
    loop(YC, b1, 1)
    fz[zh] = a_buf[zh]
    by[yc] = e_buf[:, yc]

    spread = (iota((1024, 64), 0) // 16 == iota((1024, 64), 1)).astype(BF16)
    outer = outer_ref[...].astype(BF16)

    def factors(i):
        mine = (i * 16 + iota((256, 64), 0) // 16 == iota((256, 64), 1)).astype(BF16)
        same = iota((256, 1024), 0) % 16 == iota((256, 1024), 1) % 16
        one = mm(mm(mine, outer).astype(BF16), spread, ((1,), (1,)))
        k_mat[rows(i)] = jnp.where(same, one, 0.0).astype(BF16)
        two = mm(mm(mine, outer, ((1,), (1,))).astype(BF16), spread, ((1,), (1,)))
        kt_mat[rows(i)] = jnp.where(same, two, 0.0).astype(BF16)

    loop(4, factors)

    def wide(r):
        col, row = iota((256, 1024), 1), iota((256, 1024), 0)
        place = (col // 128 * 32 + col % 32 == row) & (col % 128 // 32 == r)
        w_blk[rows(r)] = mm(blocks_ref[0], place.astype(BF16)).astype(BF16)

    loop(4, wide)

    mix = mix_ref[pl.ds(pl.multiple_of(q * 256, 256), 256)]

    def mixers(i):
        row, col = i * 256 + iota((256, 256), 0), iota((256, 256), 1)
        pick = (col == row % 32 * 8 + row // 128).astype(BF16)
        own = mm(pick, mix).astype(BF16)
        group = (iota((8, 1024), 1) // 128 == iota((8, 1024), 0)).astype(BF16)
        full = mm(own, group)
        same = iota((256, 1024), 0) % 128 == iota((256, 1024), 1) % 128
        w_mix[rows(i)] = jnp.where(same, full, 0.0).astype(BF16)

    loop(4, mixers)

    def swap(i):
        row, col = i * 128 + iota((128, 512), 0), iota((128, 512), 1)
        w_perm[rows(i, 128)] = (
            (row // 128 == col % 128 // 32) & (row % 128 // 32 == col // 128) & (row % 32 == col % 32)
        ).astype(BF16)

    loop(4, swap)

    taken(fz.at[pl.ds(0, 3)], 0)

    def f1y(d):
        to = yc_peer(d)
        put(fz.at[:, rows(to, 16)], fy.at[:, yc], 2, dev(zh, to, q))

    loop(YC, f1y, 1)
    fy[:, yc] = fz[:, rows(yc, 16)]

    taken(by.at[pl.ds(0, YC - 1)], 1)
    for hi_q in range(2):
        lanes = slice(hi_q * 128, hi_q * 128 + 128)
        t = by[:, :, :, lanes].reshape(4, 4, ZH, 16, 128)
        t = jnp.concatenate([t[:, r].reshape(256, 128) for r in range(4)], axis=1)
        t = mm(t, w_perm[...]).astype(BF16)
        for lo in range(4):
            u = t[:, lo * 128 : lo * 128 + 128].reshape(4, ZH, 16, 128)
            for hi in range(4):
                bs[:, hi_q * 4 + lo, hi] = u[hi]

    def b3(d):
        z_, q_ = plane_peer(d)
        put(bs.at[z_, q_], ba.at[q * ZH + zh], 3, dev(z_, yc, q_))

    loop(PLANE, b3, 1)
    ba[q * ZH + zh] = bs[zh, q]

    taken(fy.at[:, pl.ds(0, YC - 1)], 2)

    def second(i):
        full = mm(k_mat[rows(i)], fy[...].reshape(1024, 256))
        b_buf[rows(i)] = full
        cc[rows(i)] = (full * gate_ref[rows(i)].astype(F32)).astype(BF16)

    loop(4, second)

    def back(i):
        t = mm(kt_mat[rows(i)], cc[...]).astype(BF16).reshape(4, 4, 16, 256)
        u = jnp.concatenate([t[:, r].reshape(64, 256) for r in range(4)], axis=1)
        p = mm(u, w_blk[...]).astype(BF16)
        for g in range(NQ):
            fp[g, rows(i, 64)] = p[:, g * 128 : g * 128 + 128]

    loop(4, back)

    def f4(d):
        to = chan_peer(d)
        put(fp.at[to], fm.at[q], 4, dev(zh, yc, to))

    loop(NQ, f4, 1)
    fm[q] = fp[q]

    taken(ba.at[pl.ds(0, PLANE - 1)], 3)
    t = jnp.concatenate([ba[h * ZH : h * ZH + ZH].reshape(256, 128) for h in range(NQ)], axis=1)
    t = mm(t, w_mix[...]).astype(BF16)
    for g in range(NQ):
        bq[g] = t[:, g * 128 : g * 128 + 128]

    def b5(d):
        to = chan_peer(d)
        put(bq.at[to], bm.at[q], 5, dev(zh, yc, to))

    loop(NQ, b5, 1)
    bm[q] = bq[q]

    taken(fm.at[pl.ds(0, 7)], 4)
    t = jnp.concatenate([fm[g] for g in range(NQ)], axis=1)
    t = mm(t, w_mix[...], ((1,), (1,))).astype(BF16)
    for h in range(NQ):
        fq[h] = t[:, h * 128 : h * 128 + 128].reshape(ZH, 4, 16, 128)

    def f6(d):
        z_, q_ = plane_peer(d)
        put(fq.at[q_, z_], fa.at[zh * NQ + q], 6, dev(z_, yc, q_))

    loop(PLANE, f6, 1)
    fa[zh * NQ + q] = fq[q, zh]

    taken(bm.at[pl.ds(0, 7)], 5)

    def unmix(i):
        t = jnp.concatenate([bm[g, rows(i, 64)] for g in range(NQ)], axis=1)
        t = mm(t, w_blk[...], ((1,), (1,))).astype(BF16)
        for r in range(4):
            bd[pl.ds(i * 4, 4), r] = t[:, r * 256 : r * 256 + 256].reshape(4, 16, 256)

    loop(4, unmix)

    def third(i):
        full = mm(k_mat[rows(i)], bd[...].reshape(1024, 256))
        kgrad_ref[rows(i)] = (full * b_buf[rows(i)]).astype(BF16)
        cc[rows(i)] = (full * gate_ref[rows(i)].astype(F32)).astype(BF16)

    loop(4, third)

    def fourth(i):
        da[i] = mm(kt_mat[rows(i)], cc[...]).astype(BF16).reshape(YC, 16, 256)

    loop(4, fourth)

    def b8y(d):
        to = yc_peer(d)
        put(da.at[:, to], bt.at[:, yc], 7, dev(zh, to, q))

    loop(YC, b8y, 1)
    bt[:, yc] = da[:, yc]

    taken(fa.at[pl.ds(0, PLANE - 1)], 6)
    held = fa[...].reshape(ZH, NQ, 64, 128)
    for hi_q in range(2):
        lanes = slice(hi_q * 128, hi_q * 128 + 128)
        t = jnp.concatenate([held[:, hi_q * 4 + lo].reshape(256, 128) for lo in range(4)], axis=1)
        t = mm(t, w_perm[...]).astype(BF16)
        for r in range(4):
            u = t[:, r * 128 : r * 128 + 128].reshape(ZH, 4, 16, 128)
            for hi in range(4):
                fs[hi * 4 + r, :, :, lanes] = u[:, hi]

    def f8(d):
        to = yc_peer(d)
        put(fs.at[to], fr.at[:, yc], 8, dev(zh, to, q))

    loop(YC, f8, 1)
    fr[:, yc] = fs[yc]

    taken(bt.at[:, pl.ds(0, YC - 1)], 7)

    def b8z(d):
        to = (zh + d) % ZH
        put(bt.at[to], bu.at[zh], 9, dev(to, yc, q))

    loop(ZH, b8z, 1)
    bu[zh] = bt[zh]

    taken(fr.at[:, pl.ds(0, YC - 1)], 8)

    def last_mixed(i):
        t = mm(inner_ref[rows(i)], fr[...].reshape(1024, 256))
        mixed_ref[rows(i)] = (x_ref[rows(i)].astype(F32) + t).astype(BF16)

    loop(4, last_mixed)

    taken(bu.at[pl.ds(0, 3)], 9)

    def last_grad(i):
        t = mm(inner_ref[rows(i)], bu[...].reshape(1024, 256))
        ingrad_ref[rows(i)] = (og_ref[rows(i)].astype(F32) + t).astype(BF16)

    loop(4, last_grad)

    sent(fz.at[pl.ds(0, 3)], 0)
    sent(by.at[pl.ds(0, YC - 1)], 1)
    sent(fy.at[:, pl.ds(0, YC - 1)], 2)
    sent(ba.at[pl.ds(0, PLANE - 1)], 3)
    sent(fm.at[pl.ds(0, 7)], 4)
    sent(bm.at[pl.ds(0, 7)], 5)
    sent(fa.at[pl.ds(0, PLANE - 1)], 6)
    sent(bt.at[:, pl.ds(0, YC - 1)], 7)
    sent(fr.at[:, pl.ds(0, YC - 1)], 8)
    sent(bu.at[pl.ds(0, 3)], 9)


def local(inputs, out_grad, kernel_gate, inner_factor, outer_factor, chan_blocks, chan_mixers):
    vmem = pl.BlockSpec(memory_space=pltpu.VMEM)
    full = jax.ShapeDtypeStruct((1024, 256), BF16)

    def buf(*shape, dtype=BF16):
        return pltpu.VMEM(shape, dtype)

    mixed, in_grad, kernel_grad = pl.pallas_call(
        kernel,
        out_shape=(full, full, full),
        in_specs=[vmem] * 7,
        out_specs=(vmem, vmem, vmem),
        scratch_shapes=[
            buf(ZH, 256, 256),
            buf(ZH, YC, 16, 256),
            buf(ZH, 256, 256),
            buf(ZH, YC, 16, 256),
            buf(1024, 256, dtype=F32),
            buf(1024, 256),
            buf(NQ, 256, 128),
            buf(NQ, 256, 128),
            buf(NQ, ZH, 4, 16, 128),
            buf(PLANE, 4, 16, 128),
            buf(YC, ZH, 16, 256),
            buf(ZH, YC, 16, 256),
            buf(YC, ZH, 16, 256),
            buf(ZH, NQ, 4, 16, 128),
            buf(PLANE, 4, 16, 128),
            buf(NQ, 256, 128),
            buf(NQ, 256, 128),
            buf(16, 4, 16, 256),
            buf(ZH, YC, 16, 256),
            buf(ZH, YC, 16, 256),
            buf(ZH, YC, 16, 256),
            buf(1024, 1024),
            buf(1024, 1024),
            buf(1024, 1024),
            buf(1024, 1024),
            buf(512, 512),
            pltpu.SemaphoreType.DMA((10,)),
            pltpu.SemaphoreType.DMA((10,)),
        ],
        compiler_params=pltpu.CompilerParams(
            collective_id=0, has_side_effects=True, vmem_limit_bytes=48 << 20
        ),
    )(
        inputs,
        out_grad,
        kernel_gate.reshape(1024, 256),
        inner_factor,
        outer_factor,
        chan_blocks,
        chan_mixers.reshape(2048, 8),
    )
    return mixed, in_grad, kernel_grad.reshape(64, 16, 256)


def solution(mesh):
    in_specs = (
        P("seq", "chan"),
        P("seq", "chan"),
        P(None, "seq", "chan"),
        P(),
        P(),
        P("chan", None, None),
        P(),
    )
    out_specs = (P("seq", "chan"), P("seq", "chan"), P(None, "seq", "chan"))
    return jax.shard_map(local, mesh=mesh, in_specs=in_specs, out_specs=out_specs, check_vma=False)
```

time: 258 us -> 113 us (0.44)
  the two profiles are of different devices: /device:TPU:1 before, /device:TPU:49 now
where the time goes in v1:
time: 113 us
  Pallas kernels  102 us (90%)
  local copies, waits for them, and re-layouts  9.83 us (9%)
    pallas_call x1, Pallas kernels, local(): pl.pallas_call(kernel, out_shape=(full, full, full), in_specs=[vmem] * 7,...  102 us
    unnamed x16, local copies, waits for them, and re-layouts  9.83 us

profile of v1, /device:TPU:49, one launch (start us, length us, event | category | flops | bytes accessed | tf_op | source)
XLA Modules:
  0.0 112.8 jit_solution(1965063545001940279)
XLA Ops:
  0.6 1.1 copy.10
  1.7 0.0 copy-start
  1.7 1.6 %copy-done = bf16[1024,1024]{1,0:T(8,128)(2,1)S(1)} copy-done((bf16[1024,1024]{1,0:T(8,128)(2,1)S(1)}, bf16[1024,1024]{1,0:T(8,128)(2,1)}, u32[]{:S(2)}) %copy-start) | copy-done | bytes 2097176
  3.3 0.0 copy-start.1
  3.3 1.0 copy-done.1
  4.4 0.0 copy-start.2
  4.4 1.0 copy-done.2
  5.4 0.0 copy-start.3
  5.4 1.0 copy-done.3
  6.4 0.0 copy-start.4
  6.4 0.9 copy-done.4
  7.3 0.0 copy-start.5
  7.3 0.8 copy-done.5
  8.1 102.3 %shard_map.94 = (bf16[1024,256]{1,0:T(8,128)(2,1)S(1)}, bf16[1024,256]{1,0:T(8,128)(2,1)S(1)}, bf16[1024,256]{1,0:T(8,128)(2,1)S(1)}) custom-call(bf16[1024,256]{1,0:T(8,128)(2,1)S(1)} %copy-done.1, bf16[1024,256]{1,0:T(8,128)(2,1)S(1)} %copy-done.2, bf16[1024,256]{1,0:T(8,128)(2,1)S(1)} %bitcast.4, bf16[1024,1024]{1,0:T(8,128)(2,1)S(1)} %copy-done, ...), custom_call_target="tpu_custom_call" | custom-call | tf_op jit(solution)/shard_map/pallas_call | solution.py:327
  110.4 0.8 copy.14
  111.2 0.8 copy.15
  112.0 0.8 copy.16
Async XLA Ops:
  1.7 1.6 %copy-start = (bf16[1024,1024]{1,0:T(8,128)(2,1)S(1)}, bf16[1024,1024]{1,0:T(8,128)(2,1)}, u32[]{:S(2)}) copy-start(bf16[1024,1024]{1,0:T(8,128)(2,1)} %inner_ref.1) | copy-start | bytes 6291460
  3.3 1.0 copy-start.1
  4.4 1.0 copy-start.2
  5.4 1.0 copy-start.3
  6.4 0.9 copy-start.4
  7.3 0.8 copy-start.5

commit v2 on v0

v2 whole, which is shorter than its diff:
```python
import jax
import jax.numpy as jnp
from jax import lax
from jax.experimental import pallas as pl
from jax.experimental.pallas import tpu as pltpu
from jax.sharding import PartitionSpec as P

MESH = pl.DeviceIdType.MESH
F32 = jnp.float32
BF16 = jnp.bfloat16

ZH, YC, NX, NZ, NQ = 4, 16, 4, 8, 8
PLANE = NX * NZ
ORDER = (2, 1, 3, 0)


def mm(a, b, dims=((1,), (0,))):
    return lax.dot_general(a, b, (dims, ((), ())), preferred_element_type=F32)


def iota(shape, dim):
    return lax.broadcasted_iota(jnp.int32, shape, dim)


def kernel(
    x_hbm, og_hbm, gate_hbm, inner_hbm, outer_hbm, blocks_hbm, mix_hbm,
    mixed_hbm, ingrad_hbm, kgrad_hbm,
    a_buf, e_buf, fz, fy, b_buf, d_buf, cc, fp, fm, fq, fa, fs, fr,
    by, bs, ba, bq, bm, bd, da, bt, bu,
    k_mat, kt_mat,
    x_ref, og_ref, gate_ref, inner_ref, outer_ref, blocks_ref, mix_ref, vec_ref,
    mixed_ref, ingrad_ref, kgrad_ref,
    send, recv, load, store,
):
    s = lax.axis_index("seq")
    q = lax.axis_index("chan")
    zh, yc = s // YC, s % YC
    xx, zl = q // 2, q % 2
    zz = zh * 2 + zl

    def ahead(d):
        return (zh + d) % ZH

    def behind(d):
        return (zh + ZH - d) % ZH

    def dev(zh_, yc_, q_):
        return (zh_ * YC + yc_, q_)

    def yc_peer(d):
        y = (yc // 2 + d // 2) % 8
        return y * 2 + (yc + d) % 2

    def plane_peer(d):
        z = (zz + d // NX) % NZ
        return z // 2, ((xx + d) % NX) * 2 + z % 2

    def chan_peer(d):
        return ((xx + d // 2) % NX) * 2 + (zl + d) % 2

    def put(src, dst, stage, d, to):
        pltpu.make_async_remote_copy(
            src_ref=src, dst_ref=dst, send_sem=send.at[stage], recv_sem=recv.at[stage, d],
            device_id=to, device_id_type=MESH,
        ).start()

    near = dev(zh, yc_peer(1), q)

    def taken(part, stage, d):
        pltpu.make_async_remote_copy(
            src_ref=part, dst_ref=part, send_sem=send.at[stage], recv_sem=recv.at[stage, d],
            device_id=near, device_id_type=MESH,
        ).wait_recv()

    def sent(part, stage):
        pltpu.make_async_remote_copy(
            src_ref=part, dst_ref=part, send_sem=send.at[stage], recv_sem=recv.at[stage, 0],
            device_id=near, device_id_type=MESH,
        ).wait_send()

    def loop(n, body, start=0):
        def step(i, carry):
            body(i)
            return carry

        lax.fori_loop(start, n, step, 0)

    def rows(i, n=256):
        return pl.ds(pl.multiple_of(i * n, n), n)

    loads = [
        pltpu.make_async_copy(x_hbm, x_ref, load.at[0]),
        pltpu.make_async_copy(og_hbm, og_ref, load.at[1]),
    ]
    for i, d in enumerate(ORDER):
        loads.append(
            pltpu.make_async_copy(
                inner_hbm.at[:, rows(ahead(d))], inner_ref.at[:, rows(ahead(d))], load.at[2 + i]
            )
        )
    loads += [
        pltpu.make_async_copy(outer_hbm, outer_ref, load.at[6]),
        pltpu.make_async_copy(blocks_hbm, blocks_ref, load.at[7]),
        pltpu.make_async_copy(mix_hbm, mix_ref, load.at[8]),
        pltpu.make_async_copy(gate_hbm, gate_ref, load.at[9]),
    ]
    for copy in loads:
        copy.start()

    barrier = pltpu.get_barrier_semaphore()

    def greet_yc(d):
        pl.semaphore_signal(barrier, inc=1, device_id=dev(zh, yc_peer(d), q), device_id_type=MESH)

    def greet_plane(d):
        z_, q_ = plane_peer(d)
        pl.semaphore_signal(barrier, inc=1, device_id=dev(z_, yc, q_), device_id_type=MESH)

    loop(PLANE, greet_plane, 1)
    loop(YC, greet_yc, 1)

    def to_yc(src, dst, stage, d):
        def one(i):
            to = yc_peer(i)
            put(src(to), dst, stage, d, dev(zh, to, q))

        loop(YC, one, 1)

    def to_plane(src, dst, stage, d):
        def one(i):
            to = chan_peer(i)
            put(src(to), dst, stage, d, dev(ahead(d), yc, to))

        loop(NQ, one, 0 if d else 1)

    def to_chan(src, dst, stage, d):
        def one(i):
            to = chan_peer(i)
            put(src(to), dst, stage, d, dev(zh, yc, to))

        loop(NQ, one, 1)

    def swap(parts):
        group = iota(parts[0].shape, 1) // 32
        out = []
        for b in range(4):
            t = parts[b]
            for a in range(4):
                if a != b:
                    t = jnp.where(group == a, pltpu.roll(parts[a], (a - b) % 4 * 32, 1), t)
            out.append(t)
        return out

    loads[0].wait()
    loads[1].wait()
    for i, d in enumerate(ORDER):
        to = ahead(d)
        loads[2 + i].wait()
        tall = inner_ref[:, rows(to)]
        a_buf[to] = mm(tall, x_ref[...], ((0,), (0,))).astype(BF16)
        e_buf[to] = mm(tall, og_ref[...], ((0,), (0,))).astype(BF16).reshape(YC, 16, 256)
        if i == 0:
            pl.semaphore_wait(barrier, PLANE - 1 + YC - 1)
        if d:
            put(a_buf.at[to], fz.at[zh], 0, d, dev(to, yc, q))
        else:
            to_yc(lambda p: a_buf.at[zh, rows(p, 16)], fy.at[zh, yc], 2, 0)
            fy[zh, yc] = a_buf[zh, rows(yc, 16)]
        to_yc(lambda p, to=to: e_buf.at[to, p], by.at[yc, to], 1, d)
        by[yc, to] = e_buf[to, yc]

    for copy in loads[6:]:
        copy.wait()

    mine = (iota((256, 128), 0) == q * 32 + iota((256, 128), 1) % 32).astype(BF16)
    vec_ref[...] = mm(mix_ref[...].reshape(64, 256), mine)

    spread = (iota((1024, 64), 0) // 16 == iota((1024, 64), 1)).astype(BF16)
    outer = outer_ref[...].astype(BF16)

    def factors(i):
        mine = (i * 16 + iota((256, 64), 0) // 16 == iota((256, 64), 1)).astype(BF16)
        same = iota((256, 1024), 0) % 16 == iota((256, 1024), 1) % 16
        one = mm(mm(mine, outer).astype(BF16), spread, ((1,), (1,)))
        k_mat[rows(i)] = jnp.where(same, one, 0.0).astype(BF16)
        two = mm(mm(mine, outer, ((1,), (1,))).astype(BF16), spread, ((1,), (1,)))
        kt_mat[rows(i)] = jnp.where(same, two, 0.0).astype(BF16)

    def b2(d):
        to = ahead(d)
        taken(by.at[pl.ds(0, YC - 1), 0], 1, d)
        for hi_q in range(2):
            t = by[:, to, :, hi_q * 128 : hi_q * 128 + 128].astype(F32).reshape(4, 4, 16, 128)
            u = swap([t[:, r].reshape(64, 128) for r in range(4)])
            for lo in range(4):
                bs[to, hi_q * 4 + lo] = u[lo].astype(BF16)
        to_plane(lambda p: bs.at[to, p], ba.at[q * ZH + zh], 3, d)
        if not d:
            ba[q * ZH + zh] = bs[zh, q]

    def f1y(d):
        of = behind(d)
        taken(fz.at[0], 0, d)
        to_yc(lambda p: fz.at[of, rows(p, 16)], fy.at[of, yc], 2, d)
        fy[of, yc] = fz[of, rows(yc, 16)]

    for i, d in enumerate(ORDER):
        b2(d)
        if d:
            f1y(d)
        if i == 0:
            loop(4, factors)

    def outer_sum(out, part, of, first):
        def one(i):
            t = mm(k_mat[rows(i), rows(of)], part)
            out[rows(i)] = t if first else out[rows(i)] + t

        loop(4, one)

    def f2(d, first):
        of = behind(d)
        taken(fy.at[0, pl.ds(0, YC - 1)], 2, d)
        outer_sum(b_buf, fy[of].reshape(256, 256), of, first)

    def mixed_down(src, dst, flip):
        def one(i):
            parts = [src(g, rows(i, 16)).astype(F32) for g in range(NQ)]
            for h in range(NQ):
                t = None
                for g in range(NQ):
                    at = g * NQ + h if flip else h * NQ + g
                    u = parts[g] * vec_ref[at : at + 1]
                    t = u if t is None else t + u
                dst(h, rows(i, 16), t.astype(BF16))

        loop(4, one)

    def b4(d):
        of = behind(d)
        taken(ba.at[pl.ds(0, NQ if d else NQ - 1)], 3, d)

        def store(g, at, t):
            bq[g, of, at] = t

        mixed_down(lambda h, at: ba[h * ZH + of, at], store, True)
        to_chan(lambda p: bq.at[p, of], bm.at[q, of], 5, d)
        bm[q, of] = bq[q, of]

    f2(0, True)
    for d in ORDER[:3]:
        f2(d, False)
        b4(d)
    b4(0)

    def gated(src):
        def one(i):
            gate = gate_ref[rows(i, 16)].reshape(256, 256).astype(F32)
            cc[rows(i)] = (src[rows(i)] * gate).astype(BF16)

        loop(4, one)

    gated(b_buf)
    for d in ORDER:
        to = ahead(d)
        t = mm(kt_mat[rows(to)], cc[...]).astype(BF16)
        t = mm(t, blocks_ref[0]).reshape(4, 4, 16, 256)
        for hi_q in range(2):
            u = swap([t[:, r, :, hi_q * 128 : hi_q * 128 + 128].reshape(64, 128) for r in range(4)])
            for lo in range(4):
                fp[hi_q * 4 + lo, to] = u[lo].astype(BF16)
        to_chan(lambda p: fp.at[p, to], fm.at[q, to], 4, d)
        fm[q, to] = fp[q, to]

    def f5(d):
        to = ahead(d)
        taken(fm.at[pl.ds(0, NQ - 1), 0], 4, d)

        def store(h, at, t):
            fq[h, to, at] = t

        mixed_down(lambda g, at: fm[g, to, at], store, False)
        to_plane(lambda p: fq.at[p, to], fa.at[zh * NQ + q], 6, d)
        if not d:
            fa[zh * NQ + q] = fq[q, zh]

    def b6(d, first):
        of = behind(d)
        taken(bm.at[pl.ds(0, NQ - 1), 0], 5, d)
        half = []
        for hi_q in range(2):
            half.append(swap([bm[hi_q * 4 + lo, of].astype(F32) for lo in range(4)]))
        for r in range(4):
            t = jnp.concatenate([half[0][r], half[1][r]], axis=1).astype(BF16)
            t = mm(t, blocks_ref[0], ((1,), (1,))).astype(BF16).reshape(4, 16, 256)
            for hi in range(4):
                bd[pl.ds(hi * 64 + r * 16, 16)] = t[hi]
        outer_sum(d_buf, bd[...], of, first)

    for i, d in enumerate(ORDER):
        f5(d)
        b6(d, i == 0)

    gated(d_buf)
    for d in ORDER:
        to = ahead(d)
        da[to] = mm(kt_mat[rows(to)], cc[...]).astype(BF16).reshape(YC, 16, 256)
        to_yc(lambda p: da.at[to, p], bt.at[to, yc], 7, d)
        bt[to, yc] = da[to, yc]

    def kernel_grad(i):
        kgrad_ref[rows(i)] = (d_buf[rows(i)] * b_buf[rows(i)]).astype(BF16)

    loop(4, kernel_grad)
    out_kgrad = pltpu.make_async_copy(kgrad_ref, kgrad_hbm, store.at[8])
    out_kgrad.start()

    def f7(d):
        of = behind(d)
        taken(fa.at[pl.ds(0, NQ if d else NQ - 1)], 6, d)
        for hi_q in range(2):
            u = swap([fa[of * NQ + hi_q * 4 + lo].astype(F32) for lo in range(4)])
            for r in range(4):
                t = u[r].astype(BF16).reshape(4, 16, 128)
                for hi in range(4):
                    fs[of, hi * 4 + r, :, hi_q * 128 : hi_q * 128 + 128] = t[hi]
        to_yc(lambda p: fs.at[of, p], fr.at[of, yc], 8, d)
        fr[of, yc] = fs[of, yc]

    def b8z(d):
        to = ahead(d)
        taken(bt.at[0, pl.ds(0, YC - 1)], 7, d)
        if d:
            put(bt.at[to], bu.at[zh], 9, d, dev(to, yc, q))
        else:
            bu[zh] = bt[zh]

    for d in ORDER:
        f7(d)
        b8z(d)

    def stored(i, at):
        src, dst = ((mixed_ref, mixed_hbm), (ingrad_ref, ingrad_hbm))[at]
        return pltpu.make_async_copy(src.at[rows(i)], dst.at[rows(i)], store.at[at * 4 + i])

    def last(out, base, part, of, first, final):
        def one(i):
            t = mm(inner_ref[rows(i), rows(of)], part)
            if not first:
                t = out[rows(i)] + t
            else:
                t = base[rows(i)].astype(F32) + t
            if final is None:
                out[rows(i)] = t
            else:
                (mixed_ref, ingrad_ref)[final][rows(i)] = t.astype(BF16)
                stored(i, final).start()

        loop(4, one)

    last(d_buf, og_ref, bu[zh].reshape(256, 256), zh, True, None)
    for i, d in enumerate(ORDER):
        of = behind(d)
        taken(fr.at[0, pl.ds(0, YC - 1)], 8, d)
        last(b_buf, x_ref, fr[of].reshape(256, 256), of, i == 0, 0 if i == 3 else None)
    for i, d in enumerate(ORDER[:3]):
        of = behind(d)
        taken(bu.at[0], 9, d)
        last(d_buf, og_ref, bu[of].reshape(256, 256), of, False, 1 if i == 2 else None)

    sent(fz.at[pl.ds(0, 3)], 0)
    sent(by.at[pl.ds(0, YC - 1)], 1)
    sent(fy.at[:, pl.ds(0, YC - 1)], 2)
    sent(ba.at[pl.ds(0, PLANE - 1)], 3)
    sent(fm.at[pl.ds(0, NQ - 1)], 4)
    sent(bm.at[pl.ds(0, NQ - 1)], 5)
    sent(fa.at[pl.ds(0, PLANE - 1)], 6)
    sent(bt.at[:, pl.ds(0, YC - 1)], 7)
    sent(fr.at[:, pl.ds(0, YC - 1)], 8)
    sent(bu.at[pl.ds(0, 3)], 9)
    out_kgrad.wait()
    for i in range(4):
        stored(i, 0).wait()
        stored(i, 1).wait()


def local(inputs, out_grad, kernel_gate, inner_factor, outer_factor, chan_blocks, chan_mixers):
    full = jax.ShapeDtypeStruct((1024, 256), BF16)

    def buf(*shape, dtype=BF16):
        return pltpu.VMEM(shape, dtype)

    mixed, in_grad, kernel_grad = pl.pallas_call(
        kernel,
        out_shape=(full, full, full),
        in_specs=[pl.BlockSpec(memory_space=pl.ANY)] * 7,
        out_specs=[pl.BlockSpec(memory_space=pl.ANY)] * 3,
        scratch_shapes=[
            buf(ZH, 256, 256),
            buf(ZH, YC, 16, 256),
            buf(ZH, 256, 256),
            buf(ZH, YC, 16, 256),
            buf(1024, 256, dtype=F32),
            buf(1024, 256, dtype=F32),
            buf(1024, 256),
            buf(NQ, ZH, 64, 128),
            buf(NQ, ZH, 64, 128),
            buf(NQ, ZH, 64, 128),
            buf(PLANE, 64, 128),
            buf(ZH, YC, 16, 256),
            buf(ZH, YC, 16, 256),
            buf(YC, ZH, 16, 256),
            buf(ZH, NQ, 64, 128),
            buf(PLANE, 64, 128),
            buf(NQ, ZH, 64, 128),
            buf(NQ, ZH, 64, 128),
            buf(256, 256),
            buf(ZH, YC, 16, 256),
            buf(ZH, YC, 16, 256),
            buf(ZH, YC, 16, 256),
            buf(1024, 1024),
            buf(1024, 1024),
            buf(1024, 256),
            buf(1024, 256),
            buf(64, 16, 256),
            buf(1024, 1024),
            buf(64, 64, dtype=F32),
            buf(1, 256, 256),
            buf(8, 8, 256),
            buf(64, 128, dtype=F32),
            buf(1024, 256),
            buf(1024, 256),
            buf(1024, 256),
            pltpu.SemaphoreType.DMA((10,)),
            pltpu.SemaphoreType.DMA((10, ZH)),
            pltpu.SemaphoreType.DMA((10,)),
            pltpu.SemaphoreType.DMA((9,)),
        ],
        compiler_params=pltpu.CompilerParams(
            collective_id=0, has_side_effects=True, vmem_limit_bytes=62 << 20
        ),
    )(
        inputs,
        out_grad,
        kernel_gate,
        inner_factor,
        outer_factor,
        chan_blocks,
        jnp.transpose(chan_mixers, (1, 2, 0)),
    )
    return mixed, in_grad, kernel_grad.reshape(64, 16, 256)


def solution(mesh):
    in_specs = (
        P("seq", "chan"),
        P("seq", "chan"),
        P(None, "seq", "chan"),
        P(),
        P(),
        P("chan", None, None),
        P(),
    )
    out_specs = (P("seq", "chan"), P("seq", "chan"), P(None, "seq", "chan"))
    return jax.shard_map(local, mesh=mesh, in_specs=in_specs, out_specs=out_specs, check_vma=False)
```

time: 258 us -> 94.3 us (0.37)
  Pallas kernels: 0 us -> 88.9 us
  waiting for transfers between devices: 81.4 us -> 0 us
  blocking collectives: 47 us -> 0 us
  starting transfers between devices: 39.6 us -> 0 us
  local copies, waits for them, and re-layouts: 41.3 us -> 4.59 us
  other arithmetic: 17.2 us -> 0 us
  matrix products: 15.6 us -> 0 us
  between operations: 14.2 us -> 0.65 us
    pallas_call x0 -> x1, Pallas kernels: none -> 88.9 us  [local(): pl.pallas_call(kernel, out_shape=(full, full, full), in_specs=[pl.BlockSp...]
    all_to_all x1 -> x0, blocking collectives: 47 us -> none  [local(): lax.all_to_all(first, 'seq', split_axis=1, concat_axis=0, tiled=True)]
    all_to_all x5 -> x0, waiting for transfers between devices: 40.6 us -> none  [the longest x1 18.5 us: local(): lax.all_to_all(back, 'seq', split_axis=0, concat_axis=1, tiled=True)]
    all_gather x1 -> x0, waiting for transfers between devices: 40.1 us -> none  [local(): lax.all_gather(dq_res, 'chan', axis=1, tiled=True)]
    all_to_all x5 -> x0, starting transfers between devices: 39.6 us -> none  [the longest x1 12.1 us: local(): lax.all_to_all(dc_mat.astype(jnp.bfloat16), 'seq', split_axis=1, concat_a...]
    unnamed x31 -> x5, local copies, waits for them, and re-layouts: 27.7 us -> 4.59 us
    dot_general x9 -> x0, matrix products: 15.6 us -> none  [the longest x1 3.07 us: local(): jnp.einsum('ikc,kj->ijc', dy_grid, inner_factor, preferred_element_type=f32)]
    unnamed x4 -> x0, other arithmetic: 15.2 us -> none
  transfers between devices with their start and end apart: 6 -> 0, of which waited for: 4 -> 0; matrix products, arithmetic and copies ran while one was open for 27% -> 0% of each run, Pallas kernels for 0% -> 0%
where the time goes in v2:
time: 94.3 us; the launch traced here: 94.1 us
  Pallas kernels  88.9 us (94%)
  local copies, waits for them, and re-layouts  4.59 us (5%)
    pallas_call x1, Pallas kernels, local(): pl.pallas_call(kernel, out_shape=(full, full, full), in_specs=[pl.BlockSp...  88.9 us
    unnamed x5, local copies, waits for them, and re-layouts  4.59 us

profile of v2, /device:TPU:1, one launch (start us, length us, event | category | flops | bytes accessed | tf_op | source)
XLA Modules:
  0.0 94.1 jit_solution(12850428018026021353)
XLA Ops:
  0.6 88.9 %shard_map.94 = (bf16[1024,256]{1,0:T(8,128)(2,1)}, bf16[1024,256]{1,0:T(8,128)(2,1)}, bf16[1024,256]{1,0:T(8,128)(2,1)}) custom-call(bf16[1024,256]{1,0:T(8,128)(2,1)} %x_hbm.1, bf16[1024,256]{1,0:T(8,128)(2,1)} %og_hbm.1, bf16[64,16,256]{2,1,0:T(8,128)(2,1)} %gate_hbm.1, bf16[1024,1024]{1,0:T(8,128)(2,1)} %inner_hbm.1, f32[64,64]{1,0:T(8,128)} %outer_hbm.1, ...), custom_call_target="tpu_custom_call" | custom-call | tf_op jit(solution)/shard_map/pallas_call | solution.py:393
  89.5 0.0 copy-start
  89.5 1.9 %copy.13 = bf16[1024,256]{1,0:T(8,128)(2,1)} copy(bf16[1024,256]{1,0:T(8,128)(2,1)} %get-tuple-element.12) | data formatting | bytes 1048576
  91.5 1.9 %copy.14 = bf16[1024,256]{1,0:T(8,128)(2,1)} copy(bf16[1024,256]{1,0:T(8,128)(2,1)} %get-tuple-element.13) | data formatting | bytes 1048576
  93.3 0.0 copy-done
  93.3 0.8 copy.15
Async XLA Ops:
  89.5 3.8 %copy-start = (bf16[1024,256]{1,0:T(8,128)(2,1)S(1)}, bf16[1024,256]{1,0:T(8,128)(2,1)}, u32[]{:S(2)}) copy-start(bf16[1024,256]{1,0:T(8,128)(2,1)} %get-tuple-element.8) | copy-start | bytes 1572868

commit v3 on v2

--- a/solution.py
+++ b/solution.py
@@ -11,7 +11,7 @@
 
 ZH, YC, NX, NZ, NQ = 4, 16, 4, 8, 8
 PLANE = NX * NZ
-ORDER = (2, 1, 3, 0)
+ORDER = (1, 3, 2, 0)
 
 
 def mm(a, b, dims=((1,), (0,))):
@@ -34,29 +34,17 @@
 ):
     s = lax.axis_index("seq")
     q = lax.axis_index("chan")
-    zh, yc = s // YC, s % YC
-    xx, zl = q // 2, q % 2
-    zz = zh * 2 + zl
+    zh, yc = s >> 4, s & 15
+    xx, zl = q >> 1, q & 1
 
     def ahead(d):
-        return (zh + d) % ZH
+        return (zh + d) & (ZH - 1)
 
     def behind(d):
-        return (zh + ZH - d) % ZH
+        return (zh + ZH - d) & (ZH - 1)
 
     def dev(zh_, yc_, q_):
         return (zh_ * YC + yc_, q_)
-
-    def yc_peer(d):
-        y = (yc // 2 + d // 2) % 8
-        return y * 2 + (yc + d) % 2
-
-    def plane_peer(d):
-        z = (zz + d // NX) % NZ
-        return z // 2, ((xx + d) % NX) * 2 + z % 2
-
-    def chan_peer(d):
-        return ((xx + d // 2) % NX) * 2 + (zl + d) % 2
 
     def put(src, dst, stage, d, to):
         pltpu.make_async_remote_copy(
@@ -64,7 +52,7 @@
             device_id=to, device_id_type=MESH,
         ).start()
 
-    near = dev(zh, yc_peer(1), q)
+    near = (s ^ 1, q)
 
     def taken(part, stage, d):
         pltpu.make_async_remote_copy(
@@ -109,33 +97,30 @@
 
     barrier = pltpu.get_barrier_semaphore()
 
-    def greet_yc(d):
-        pl.semaphore_signal(barrier, inc=1, device_id=dev(zh, yc_peer(d), q), device_id_type=MESH)
-
-    def greet_plane(d):
-        z_, q_ = plane_peer(d)
-        pl.semaphore_signal(barrier, inc=1, device_id=dev(z_, yc, q_), device_id_type=MESH)
-
-    loop(PLANE, greet_plane, 1)
-    loop(YC, greet_yc, 1)
+    def greet(seq, chan):
+        pl.semaphore_signal(barrier, inc=1, device_id=(seq, chan), device_id_type=MESH)
+
+    for z in range(1, ZH):
+        loop(NQ, lambda i, z=z: greet(s ^ z * YC, q ^ i))
+    loop(NQ, lambda i: greet(s, q ^ i), 1)
+    loop(YC, lambda i: greet(s ^ i, q), 1)
 
     def to_yc(src, dst, stage, d):
         def one(i):
-            to = yc_peer(i)
-            put(src(to), dst, stage, d, dev(zh, to, q))
+            put(src(yc ^ i), dst, stage, d, (s ^ i, q))
 
         loop(YC, one, 1)
 
     def to_plane(src, dst, stage, d):
         def one(i):
-            to = chan_peer(i)
+            to = q ^ i
             put(src(to), dst, stage, d, dev(ahead(d), yc, to))
 
         loop(NQ, one, 0 if d else 1)
 
     def to_chan(src, dst, stage, d):
         def one(i):
-            to = chan_peer(i)
+            to = q ^ i
             put(src(to), dst, stage, d, dev(zh, yc, to))
 
         loop(NQ, one, 1)
@@ -363,7 +348,7 @@
         of = behind(d)
         taken(fr.at[0, pl.ds(0, YC - 1)], 8, d)
         last(b_buf, x_ref, fr[of].reshape(256, 256), of, i == 0, 0 if i == 3 else None)
-    for i, d in enumerate(ORDER[:3]):
+    for i, d in enumerate([d for d in ORDER if d]):
         of = behind(d)
         taken(bu.at[0], 9, d)
         last(d_buf, og_ref, bu[of].reshape(256, 256), of, False, 1 if i == 2 else None)
@@ -382,6 +367,19 @@
     for i in range(4):
         stored(i, 0).wait()
         stored(i, 1).wait()
+
+
+def hand_on(a_src, b_src, c_src, a_dst, b_dst, c_dst, held, come, go):
+    pairs = ((c_src, c_dst), (a_src, a_dst), (b_src, b_dst))
+    into = [pltpu.make_async_copy(p[0], held.at[i], come.at[i]) for i, p in enumerate(pairs)]
+    out = [pltpu.make_async_copy(held.at[i], p[1], go.at[i]) for i, p in enumerate(pairs)]
+    for copy in into:
+        copy.start()
+    for one, two in zip(into, out):
+        one.wait()
+        two.start()
+    for copy in out:
+        copy.wait()
 
 
 def local(inputs, out_grad, kernel_gate, inner_factor, outer_factor, chan_blocks, chan_mixers):
@@ -448,6 +446,14 @@
         chan_blocks,
         jnp.transpose(chan_mixers, (1, 2, 0)),
     )
+    mixed, in_grad, kernel_grad = pl.pallas_call(
+        hand_on,
+        out_shape=(full, full, full),
+        in_specs=[pl.BlockSpec(memory_space=pl.ANY)] * 3,
+        out_specs=[pl.BlockSpec(memory_space=pl.ANY)] * 3,
+        scratch_shapes=[buf(3, 1024, 256), pltpu.SemaphoreType.DMA((3,)), pltpu.SemaphoreType.DMA((3,))],
+        compiler_params=pltpu.CompilerParams(vmem_limit_bytes=62 << 20),
+    )(mixed, in_grad, kernel_grad)
     return mixed, in_grad, kernel_grad.reshape(64, 16, 256)
 
 

time: 94.3 us -> 89 us (0.944)
  local copies, waits for them, and re-layouts: 4.59 us -> 0 us
    unnamed x5 -> x0, local copies, waits for them, and re-layouts: 4.59 us -> none
    pallas_call x1, Pallas kernels: 88.9 us -> 86 us  [local(): pl.pallas_call(kernel, out_shape=(full, full, full), in_specs=[pl.BlockSp...]
    pallas_call x0 -> x1, Pallas kernels: none -> 2.23 us  [local(): pl.pallas_call(hand_on, out_shape=(full, full, full), in_specs=[pl.BlockS...]
where the time goes in v3:
time: 89 us; the launch traced here: 88.9 us
  Pallas kernels  88.2 us (99%)
    pallas_call x1, Pallas kernels, local(): pl.pallas_call(kernel, out_shape=(full, full, full), in_specs=[pl.BlockSp...  86 us
    pallas_call x1, Pallas kernels, local(): pl.pallas_call(hand_on, out_shape=(full, full, full), in_specs=[pl.BlockS...  2.23 us

profile of v3, /device:TPU:1, one launch (start us, length us, event | category | flops | bytes accessed | tf_op | source)
XLA Modules:
  0.0 88.9 jit_solution(7639856561076063268)
XLA Ops:
  0.6 86.0 %shard_map.94 = (bf16[1024,256]{1,0:T(8,128)(2,1)}, bf16[1024,256]{1,0:T(8,128)(2,1)}, bf16[1024,256]{1,0:T(8,128)(2,1)}) custom-call(bf16[1024,256]{1,0:T(8,128)(2,1)} %x_hbm.1, bf16[1024,256]{1,0:T(8,128)(2,1)} %og_hbm.1, bf16[64,16,256]{2,1,0:T(8,128)(2,1)} %gate_hbm.1, bf16[1024,1024]{1,0:T(8,128)(2,1)} %inner_hbm.1, f32[64,64]{1,0:T(8,128)} %outer_hbm.1, ...), custom_call_target="tpu_custom_call" | custom-call | tf_op jit(solution)/shard_map/pallas_call | solution.py:391
  86.6 2.2 %shard_map.95 = (bf16[1024,256]{1,0:T(8,128)(2,1)}, bf16[1024,256]{1,0:T(8,128)(2,1)}, bf16[1024,256]{1,0:T(8,128)(2,1)}) custom-call(bf16[1024,256]{1,0:T(8,128)(2,1)} %get-tuple-element.9.a_src, bf16[1024,256]{1,0:T(8,128)(2,1)} %get-tuple-element.10.b_src, bf16[1024,256]{1,0:T(8,128)(2,1)} %get-tuple-element.11.c_src), custom_call_target="tpu_custom_call" | custom-call | tf_op jit(solution)/shard_map/pallas_call | solution.py:449

commit v4 on v3

--- a/solution.py
+++ b/solution.py
@@ -28,7 +28,7 @@
     a_buf, e_buf, fz, fy, b_buf, d_buf, cc, fp, fm, fq, fa, fs, fr,
     by, bs, ba, bq, bm, bd, da, bt, bu,
     k_mat, kt_mat,
-    x_ref, og_ref, gate_ref, inner_ref, outer_ref, blocks_ref, mix_ref, vec_ref,
+    both_ref, gate_ref, inner_ref, outer_ref, blocks_ref, mix_ref, vec_ref,
     mixed_ref, ingrad_ref, kgrad_ref,
     send, recv, load, store,
 ):
@@ -36,6 +36,9 @@
     q = lax.axis_index("chan")
     zh, yc = s >> 4, s & 15
     xx, zl = q >> 1, q & 1
+
+    x_ref = both_ref.at[:, pl.ds(0, 256)]
+    og_ref = both_ref.at[:, pl.ds(256, 256)]
 
     def ahead(d):
         return (zh + d) & (ZH - 1)
@@ -142,8 +145,9 @@
         to = ahead(d)
         loads[2 + i].wait()
         tall = inner_ref[:, rows(to)]
-        a_buf[to] = mm(tall, x_ref[...], ((0,), (0,))).astype(BF16)
-        e_buf[to] = mm(tall, og_ref[...], ((0,), (0,))).astype(BF16).reshape(YC, 16, 256)
+        t = mm(tall, both_ref[...], ((0,), (0,))).astype(BF16)
+        a_buf[to] = t[:, :256]
+        e_buf[to] = t[:, 256:].reshape(YC, 16, 256)
         if i == 0:
             pl.semaphore_wait(barrier, PLANE - 1 + YC - 1)
         if d:
@@ -196,17 +200,20 @@
         if i == 0:
             loop(4, factors)
 
-    def outer_sum(out, part, of, first):
+    def outer_sum(out, part, of, first, final=False):
         def one(i):
             t = mm(k_mat[rows(i), rows(of)], part)
-            out[rows(i)] = t if first else out[rows(i)] + t
+            t = t if first else out[rows(i)] + t
+            out[rows(i)] = t
+            if final:
+                cc[rows(i)] = (t * gate_ref[rows(i, 16)].reshape(256, 256).astype(F32)).astype(BF16)
 
         loop(4, one)
 
-    def f2(d, first):
+    def f2(d, first, final=False):
         of = behind(d)
         taken(fy.at[0, pl.ds(0, YC - 1)], 2, d)
-        outer_sum(b_buf, fy[of].reshape(256, 256), of, first)
+        outer_sum(b_buf, fy[of].reshape(256, 256), of, first, final)
 
     def mixed_down(src, dst, flip):
         def one(i):
@@ -234,18 +241,10 @@
 
     f2(0, True)
     for d in ORDER[:3]:
-        f2(d, False)
+        f2(d, False, d == 2)
         b4(d)
     b4(0)
 
-    def gated(src):
-        def one(i):
-            gate = gate_ref[rows(i, 16)].reshape(256, 256).astype(F32)
-            cc[rows(i)] = (src[rows(i)] * gate).astype(BF16)
-
-        loop(4, one)
-
-    gated(b_buf)
     for d in ORDER:
         to = ahead(d)
         t = mm(kt_mat[rows(to)], cc[...]).astype(BF16)
@@ -269,7 +268,7 @@
         if not d:
             fa[zh * NQ + q] = fq[q, zh]
 
-    def b6(d, first):
+    def b6(d, first, final):
         of = behind(d)
         taken(bm.at[pl.ds(0, NQ - 1), 0], 5, d)
         half = []
@@ -280,13 +279,12 @@
             t = mm(t, blocks_ref[0], ((1,), (1,))).astype(BF16).reshape(4, 16, 256)
             for hi in range(4):
                 bd[pl.ds(hi * 64 + r * 16, 16)] = t[hi]
-        outer_sum(d_buf, bd[...], of, first)
+        outer_sum(d_buf, bd[...], of, first, final)
 
     for i, d in enumerate(ORDER):
+        b6(d, i == 0, i == 3)
         f5(d)
-        b6(d, i == 0)
-
-    gated(d_buf)
+
     for d in ORDER:
         to = ahead(d)
         da[to] = mm(kt_mat[rows(to)], cc[...]).astype(BF16).reshape(YC, 16, 256)
@@ -321,8 +319,8 @@
             bu[zh] = bt[zh]
 
     for d in ORDER:
+        b8z(d)
         f7(d)
-        b8z(d)
 
     def stored(i, at):
         src, dst = ((mixed_ref, mixed_hbm), (ingrad_ref, ingrad_hbm))[at]
@@ -343,15 +341,24 @@
 
         loop(4, one)
 
+    def f9(d, first, final):
+        of = behind(d)
+        taken(fr.at[0, pl.ds(0, YC - 1)], 8, d)
+        last(b_buf, x_ref, fr[of].reshape(256, 256), of, first, final)
+
+    def b9(d, final):
+        of = behind(d)
+        taken(bu.at[0], 9, d)
+        last(d_buf, og_ref, bu[of].reshape(256, 256), of, False, final)
+
     last(d_buf, og_ref, bu[zh].reshape(256, 256), zh, True, None)
-    for i, d in enumerate(ORDER):
-        of = behind(d)
-        taken(fr.at[0, pl.ds(0, YC - 1)], 8, d)
-        last(b_buf, x_ref, fr[of].reshape(256, 256), of, i == 0, 0 if i == 3 else None)
-    for i, d in enumerate([d for d in ORDER if d]):
-        of = behind(d)
-        taken(bu.at[0], 9, d)
-        last(d_buf, og_ref, bu[of].reshape(256, 256), of, False, 1 if i == 2 else None)
+    f9(1, True, None)
+    f9(3, False, None)
+    b9(1, None)
+    f9(2, False, None)
+    b9(3, None)
+    f9(0, False, 0)
+    b9(2, 1)
 
     sent(fz.at[pl.ds(0, 3)], 0)
     sent(by.at[pl.ds(0, YC - 1)], 1)
@@ -370,7 +377,11 @@
 
 
 def hand_on(a_src, b_src, c_src, a_dst, b_dst, c_dst, held, come, go):
-    pairs = ((c_src, c_dst), (a_src, a_dst), (b_src, b_dst))
+    pairs = [
+        (src.at[pl.ds(k * 256, 256)], dst.at[pl.ds(k * 256, 256)])
+        for src, dst in ((c_src, c_dst), (a_src, a_dst), (b_src, b_dst))
+        for k in range(4)
+    ]
     into = [pltpu.make_async_copy(p[0], held.at[i], come.at[i]) for i, p in enumerate(pairs)]
     out = [pltpu.make_async_copy(held.at[i], p[1], go.at[i]) for i, p in enumerate(pairs)]
     for copy in into:
@@ -418,8 +429,7 @@
             buf(ZH, YC, 16, 256),
             buf(1024, 1024),
             buf(1024, 1024),
-            buf(1024, 256),
-            buf(1024, 256),
+            buf(1024, 512),
             buf(64, 16, 256),
             buf(1024, 1024),
             buf(64, 64, dtype=F32),
@@ -451,7 +461,7 @@
         out_shape=(full, full, full),
         in_specs=[pl.BlockSpec(memory_space=pl.ANY)] * 3,
         out_specs=[pl.BlockSpec(memory_space=pl.ANY)] * 3,
-        scratch_shapes=[buf(3, 1024, 256), pltpu.SemaphoreType.DMA((3,)), pltpu.SemaphoreType.DMA((3,))],
+        scratch_shapes=[buf(12, 256, 256), pltpu.SemaphoreType.DMA((12,)), pltpu.SemaphoreType.DMA((12,))],
         compiler_params=pltpu.CompilerParams(vmem_limit_bytes=62 << 20),
     )(mixed, in_grad, kernel_grad)
     return mixed, in_grad, kernel_grad.reshape(64, 16, 256)

time: 89 us -> 87.3 us (0.981); the launches traced: 88.9 us -> 86.1 us
  Pallas kernels: 88.2 us -> 85.4 us
    pallas_call x1, Pallas kernels: 86 us -> 83.1 us  [local(): pl.pallas_call(kernel, out_shape=(full, full, full), in_specs=[pl.BlockSp...]
where the time goes in v4:
time: 87.3 us; the launch traced here: 86.1 us
  Pallas kernels  85.4 us (98%)
    pallas_call x1, Pallas kernels, local(): pl.pallas_call(kernel, out_shape=(full, full, full), in_specs=[pl.BlockSp...  83.1 us
    pallas_call x1, Pallas kernels, local(): pl.pallas_call(hand_on, out_shape=(full, full, full), in_specs=[pl.BlockS...  2.33 us

profile of v4, /device:TPU:1, one launch (start us, length us, event | category | flops | bytes accessed | tf_op | source)
XLA Modules:
  0.0 86.1 jit_solution(7192165378151631112)
XLA Ops:
  0.6 83.1 %shard_map.94 = (bf16[1024,256]{1,0:T(8,128)(2,1)}, bf16[1024,256]{1,0:T(8,128)(2,1)}, bf16[1024,256]{1,0:T(8,128)(2,1)}) custom-call(bf16[1024,256]{1,0:T(8,128)(2,1)} %x_hbm.1, bf16[1024,256]{1,0:T(8,128)(2,1)} %og_hbm.1, bf16[64,16,256]{2,1,0:T(8,128)(2,1)} %gate_hbm.1, bf16[1024,1024]{1,0:T(8,128)(2,1)} %inner_hbm.1, f32[64,64]{1,0:T(8,128)} %outer_hbm.1, ...), custom_call_target="tpu_custom_call" | custom-call | tf_op jit(solution)/shard_map/pallas_call | solution.py:402
  83.8 2.3 %shard_map.95 = (bf16[1024,256]{1,0:T(8,128)(2,1)}, bf16[1024,256]{1,0:T(8,128)(2,1)}, bf16[1024,256]{1,0:T(8,128)(2,1)}) custom-call(bf16[1024,256]{1,0:T(8,128)(2,1)} %get-tuple-element.9.a_src, bf16[1024,256]{1,0:T(8,128)(2,1)} %get-tuple-element.10.b_src, bf16[1024,256]{1,0:T(8,128)(2,1)} %get-tuple-element.11.c_src), custom_call_target="tpu_custom_call" | custom-call | tf_op jit(solution)/shard_map/pallas_call | solution.py:459

commit v5 on v4

--- a/solution.py
+++ b/solution.py
@@ -197,7 +197,7 @@
         b2(d)
         if d:
             f1y(d)
-        if i == 0:
+        if i == 1:
             loop(4, factors)
 
     def outer_sum(out, part, of, first, final=False):

time: 87.3 us -> 85.6 us (0.981); the launches traced: 86.1 us -> 85.5 us
  no operation moved by 1% of the time
where the time goes in v5:
time: 85.6 us; the launch traced here: 85.5 us
  Pallas kernels  84.8 us (99%)
    pallas_call x1, Pallas kernels, local(): pl.pallas_call(kernel, out_shape=(full, full, full), in_specs=[pl.BlockSp...  82.5 us
    pallas_call x1, Pallas kernels, local(): pl.pallas_call(hand_on, out_shape=(full, full, full), in_specs=[pl.BlockS...  2.33 us

profile of v5, /device:TPU:1, one launch (start us, length us, event | category | flops | bytes accessed | tf_op | source)
XLA Modules:
  0.0 85.5 jit_solution(14101693619451519399)
XLA Ops:
  0.6 82.5 %shard_map.94 = (bf16[1024,256]{1,0:T(8,128)(2,1)}, bf16[1024,256]{1,0:T(8,128)(2,1)}, bf16[1024,256]{1,0:T(8,128)(2,1)}) custom-call(bf16[1024,256]{1,0:T(8,128)(2,1)} %x_hbm.1, bf16[1024,256]{1,0:T(8,128)(2,1)} %og_hbm.1, bf16[64,16,256]{2,1,0:T(8,128)(2,1)} %gate_hbm.1, bf16[1024,1024]{1,0:T(8,128)(2,1)} %inner_hbm.1, f32[64,64]{1,0:T(8,128)} %outer_hbm.1, ...), custom_call_target="tpu_custom_call" | custom-call | tf_op jit(solution)/shard_map/pallas_call | solution.py:402
  83.2 2.3 %shard_map.95 = (bf16[1024,256]{1,0:T(8,128)(2,1)}, bf16[1024,256]{1,0:T(8,128)(2,1)}, bf16[1024,256]{1,0:T(8,128)(2,1)}) custom-call(bf16[1024,256]{1,0:T(8,128)(2,1)} %get-tuple-element.9.a_src, bf16[1024,256]{1,0:T(8,128)(2,1)} %get-tuple-element.10.b_src, bf16[1024,256]{1,0:T(8,128)(2,1)} %get-tuple-element.11.c_src), custom_call_target="tpu_custom_call" | custom-call | tf_op jit(solution)/shard_map/pallas_call | solution.py:459
